TPU v7x, 32 devices: a whole 2x2x4 slice. The times are simulated.
32 devices in a mesh: ctx: 8 (over z, y), head: 4 (over x, core).
Axes of the slice: x: 2, y: 2, z: 4, core: 2. Of those that a mesh axis runs over, the one named last changes fastest.
Arguments:
- prompt_hidden: bfloat16 [4, 4096, 5120], P(None, 'ctx', 'head'), may hold values from -6 to 6
- prompt_lengths: int32 [4], replicated, may hold values from 2048 to 4096, as said below
- group_prompt: int32 [8], replicated, may hold values from 0 to 3, as said below
- sample_hidden: bfloat16 [8, 4, 16, 5120], P('ctx'), may hold values from -6 to 6
- norm_gain: float32 [5120], replicated, may hold values from 0.1 to 1.9
- q_gain: float32 [128], replicated, may hold values from 0.5 to 6
- k_gain: float32 [128], replicated, may hold values from 0.5 to 6
- w_q: bfloat16 [5120, 8192], P('ctx', 'head'), may hold values from -0.078125 to 0.078125
- w_kv: bfloat16 [5120, 2, 1024], P(None, None, 'head'), may hold values from -0.078125 to 0.078125
- w_o: bfloat16 [8192, 5120], P('head', 'ctx'), may hold values from -0.375 to 0.375
Outputs:
- decoded: bfloat16 [8, 4, 16, 5120], P('ctx', None, None, 'head')
- kv_cache: bfloat16 [8, 4096, 2, 1024], P('ctx', None, None, 'head')
Inputs may be any that keep to these rules, and one draw needn't show every extreme that they name: `prompt_lengths`: one prompt has exactly 4096 live positions and another exactly 2048. `group_prompt`: each prompt is sampled by exactly 2 groups.
All inputs are finite; a program needn't handle non-finite values.
Results may differ from a plain program's by a relative error of at most 0.007.
The roundings to bfloat16 on the way count: a program that leaves them out, or rounds other values in their place, can miss the bound.
Values may be sent and summed in bfloat16 or wider, within the bound.
A program may use at most 256 MiB of HBM per device.

v0:
```python
import jax
import jax.numpy as jnp
from jax import lax
from jax.sharding import PartitionSpec as P

EPS = 1e-06
THETA = 1000000.0


def rotary(vector, position):
    half_size = vector.shape[-1] // 2
    frequency = THETA ** (-jnp.arange(half_size, dtype=jnp.float32) * 2.0 / vector.shape[-1])
    angle = position[..., None] * frequency
    cosine = jnp.cos(angle)
    sine = jnp.sin(angle)
    first = vector[..., :half_size]
    second = vector[..., half_size:]
    return jnp.concatenate([first * cosine - second * sine, second * cosine + first * sine], -1)


def head_norm(vector, gain):
    return vector * lax.rsqrt(jnp.mean(vector * vector, -1, keepdims=True) + EPS) * gain


def attend(queries, prefix_keys, prefix_values, new_keys, new_values, length, samples):
    total_rows = queries.shape[0]
    prefix_scores = jnp.einsum(
        "rkgd,lkd->kgrl", queries, prefix_keys, preferred_element_type=jnp.float32
    )
    suffix_scores = jnp.einsum(
        "rkgd,ukd->kgru", queries, new_keys, preferred_element_type=jnp.float32
    )
    live = jnp.arange(prefix_keys.shape[0]) < length
    prefix_scores = jnp.where(live, prefix_scores, -1e30)
    row_index = jnp.arange(total_rows)
    same_sample = row_index[:, None] % samples == row_index[None, :] % samples
    earlier = row_index[None, :] // samples <= row_index[:, None] // samples
    suffix_scores = jnp.where(same_sample & earlier, suffix_scores, -1e30)
    top = jnp.maximum(
        jnp.max(prefix_scores, -1, keepdims=True), jnp.max(suffix_scores, -1, keepdims=True)
    )
    prefix_exp = jnp.exp(prefix_scores - top)
    suffix_exp = jnp.exp(suffix_scores - top)
    total = jnp.sum(prefix_exp, -1, keepdims=True) + jnp.sum(suffix_exp, -1, keepdims=True)
    prefix_weight = (prefix_exp / total).astype(jnp.bfloat16)
    suffix_weight = (suffix_exp / total).astype(jnp.bfloat16)
    result = jnp.einsum(
        "kgrl,lkd->rkgd", prefix_weight, prefix_values, preferred_element_type=jnp.float32
    )
    result = result + jnp.einsum(
        "kgru,ukd->rkgd", suffix_weight, new_values, preferred_element_type=jnp.float32
    )
    return result.reshape(total_rows, -1).astype(jnp.bfloat16)


def local(
    prompt_hidden,
    prompt_lengths,
    group_prompt,
    sample_hidden,
    norm_gain,
    q_gain,
    k_gain,
    w_q,
    w_kv,
    w_o,
):
    prompts, slab, part_width = prompt_hidden.shape
    model_width = norm_gain.shape[0]
    head_dim = q_gain.shape[0]
    kv_width = w_kv.shape[2]
    kv_local = kv_width // head_dim
    q_width = w_q.shape[1]
    q_local = q_width // head_dim
    group_size = q_local // kv_local
    ctx_index = lax.axis_index("ctx")
    prompt_rows = prompts * slab
    flat_weights = w_kv.reshape(model_width, 2 * kv_width)
    piece = lax.all_gather(prompt_hidden, "head", axis=2, tiled=True)
    count = piece.shape[2]
    wide_piece = piece.astype(jnp.float32).reshape(prompt_rows, count)
    scaled_piece = (wide_piece * norm_gain).astype(jnp.bfloat16)
    running_sum = jnp.dot(scaled_piece, flat_weights, preferred_element_type=jnp.float32)
    squares = jnp.sum(wide_piece * wide_piece, -1)
    prefill_inverse = lax.rsqrt(squares / model_width + EPS)[:, None]
    raw = (running_sum * prefill_inverse).reshape(prompts, slab, 2, kv_local, head_dim)
    positions = (ctx_index * slab + jnp.arange(slab, dtype=jnp.int32)).astype(jnp.float32)
    prompt_keys = rotary(head_norm(raw[:, :, 0], k_gain), positions[None, :, None])
    cache_local = jnp.stack([prompt_keys, raw[:, :, 1]], 2).astype(jnp.bfloat16)
    cache_local = cache_local.reshape(prompts, slab, 2, kv_width)
    ordered = jnp.take(cache_local, group_prompt, axis=0)
    kv_cache = lax.all_to_all(ordered, "ctx", split_axis=0, concat_axis=1, tiled=True)
    length = jnp.take(prompt_lengths, jnp.take(group_prompt, ctx_index))
    steps = sample_hidden.shape[1]
    samples = sample_hidden.shape[2]
    token_rows = steps * samples
    wide = sample_hidden.reshape(token_rows, model_width).astype(jnp.float32)
    token_inverse = lax.rsqrt(jnp.mean(wide * wide, -1) + EPS)[:, None]
    token_scaled = (wide * norm_gain).astype(jnp.bfloat16)
    queries = jnp.dot(
        token_scaled,
        lax.all_gather(w_q, "ctx", axis=0, tiled=True),
        preferred_element_type=jnp.float32,
    )
    queries = queries * token_inverse
    fresh = jnp.dot(token_scaled, flat_weights, preferred_element_type=jnp.float32) * token_inverse
    fresh = fresh.reshape(token_rows, 2, kv_local, head_dim)
    row_position = jnp.repeat(length + jnp.arange(steps, dtype=jnp.int32), samples).astype(
        jnp.float32
    )
    queries = rotary(
        head_norm(queries.reshape(token_rows, q_local, head_dim), q_gain), row_position[:, None]
    )
    queries = (queries * head_dim ** (-0.5)).astype(jnp.bfloat16)
    queries = queries.reshape(token_rows, kv_local, group_size, head_dim)
    new_keys = rotary(head_norm(fresh[:, 0], k_gain), row_position[:, None]).astype(jnp.bfloat16)
    new_values = fresh[:, 1].astype(jnp.bfloat16)
    prefix_keys = kv_cache[0, :, 0].reshape(-1, kv_local, head_dim)
    prefix_values = kv_cache[0, :, 1].reshape(-1, kv_local, head_dim)
    attended = attend(queries, prefix_keys, prefix_values, new_keys, new_values, length, samples)
    partial_out = jnp.dot(
        attended, lax.all_gather(w_o, "ctx", axis=1, tiled=True), preferred_element_type=jnp.float32
    )
    summed = lax.psum_scatter(partial_out, "head", scatter_dimension=1, tiled=True)
    out_width = summed.shape[1]
    residual = lax.dynamic_slice_in_dim(wide, lax.axis_index("head") * out_width, out_width, 1)
    decoded = (residual + summed).astype(jnp.bfloat16).reshape(1, steps, samples, out_width)
    return (decoded, kv_cache)


def solution(mesh):
    return jax.shard_map(
        local,
        mesh=mesh,
        in_specs=(
            P(None, "ctx", "head"),
            P(),
            P(),
            P("ctx", None, None, None),
            P(),
            P(),
            P(),
            P("ctx", "head"),
            P(None, None, "head"),
            P("head", "ctx"),
        ),
        out_specs=(P("ctx", None, None, "head"), P("ctx", None, None, "head")),
        check_vma=False,
    )
```

profile of v0, /device:TPU:3, one launch (start us, length us, event | category | flops | bytes accessed | tf_op | source)
XLA Modules:
  0.0 1039.8 jit_solution(8636083225317817277)
XLA Ops:
  9.4 5.7 copy.78
  15.2 1.0 multiply_cosine_fusion
  16.2 125.5 %all-gather.4.cloned.1.call-done = bf16[4,512,5120]{2,1,0:T(8,128)(2,1)} async-done(((bf16[4,512,1280]{2,1,0:T(8,128)(2,1)}), bf16[4,512,5120]{2,1,0:T(8,128)(2,1)}) %all-gather.4.cloned.1.call-update) | async-done | bytes 20971536 | tf_op jit(solution)/shard_map/all_gather | solution.py:79
  141.7 20.0 %fusion.1 = (f32[4,512]{1,0:T(4,128)S(1)}, bf16[4,512,5120]{2,1,0:T(8,128)(2,1)}) fusion(bf16[4,512,5120]{2,1,0:T(8,128)(2,1)} %all-gather.4.cloned.1.call-done, f32[5120]{0:T(1024)S(1)} %copy-done.7), kind=kLoop, calls=%fused_computation.4 | loop fusion | flops 52426752 | bytes 41971712 | tf_op jit(solution)/shard_map/reduce_sum | solution.py:84
  161.8 16.6 %convolution_multiply_fusion = f32[2048,512]{1,0:T(8,128)} fusion(bf16[2048,5120]{1,0:T(8,128)(2,1)} %bitcast.94, bf16[5120,512]{1,0:T(8,128)(2,1)S(1)} %bitcast.93, f32[2048]{0:T(1024)S(1)} %bitcast.104), kind=kOutput, calls=%fused_computation.12 | convolution fusion | flops 10738466816 | bytes 30416896 | tf_op jit(solution)/shard_map/dot_general | solution.py:83
  178.3 5.9 reshape.375
  184.2 2.5 slice.92
  186.7 3.9 multiply_reduce_fusion
  190.7 3.0 multiply_multiply_fusion
  193.8 2.9 subtract_convert_fusion
  196.7 2.9 pad_maximum_fusion.1
  200.3 1.5 stack.9
  201.8 1.4 pad_maximum_fusion
  203.2 2.8 gather_fusion
  206.0 4.7 broadcast_select_fusion
  210.7 5.5 all-to-all-start
  217.2 3.6 convolution_multiply_fusion.2
  223.8 366.9 %all-gather.6.cloned.1.call-done = bf16[5120,2048]{1,0:T(8,128)(2,1)} async-done(((bf16[640,2048]{1,0:T(8,128)(2,1)}), bf16[5120,2048]{1,0:T(8,128)(2,1)}) %all-gather.6.cloned.1.call-update) | async-done | bytes 20971536 | tf_op jit(solution)/shard_map/all_gather | solution.py:102
  590.7 8.9 fusion.6
  601.7 1.2 fusion.24
  602.9 2.5 copy.54
  605.4 2.5 fusion.23
  608.6 2.9 copy.56
  611.6 4.1 copy.55
  615.6 9.2 bitcast_reduce_fusion
  625.0 9.1 fusion.3
  634.1 7.9 fusion.4
  642.5 351.6 %all-gather.8.cloned.1.call-done = bf16[2048,5120]{1,0:T(8,128)(2,1)} async-done(((bf16[2048,640]{1,0:T(8,128)(2,1)}), bf16[2048,5120]{1,0:T(8,128)(2,1)}) %all-gather.8.cloned.1.call-update) | async-done | bytes 20971536 | tf_op jit(solution)/shard_map/all_gather | solution.py:122
  994.1 11.8 %fusion.12 = f32[64,5120]{1,0:T(8,128)} fusion(bf16[2048,5120]{1,0:T(8,128)(2,1)} %all-gather.8.cloned.1.call-done, bf16[8,8,16,128]{3,2,1,0:T(8,128)(2,1)S(1)} %bitcast.102), kind=kOutput, calls=%fused_computation.46 | convolution fusion | flops 1342177280 | bytes 22544384 | tf_op jit(solution)/shard_map/dot_general | solution.py:121
  1005.9 10.2 copy.65
  1016.1 15.5 %reduce-scatter.2.cloned.1.call-done = f32[64,1280]{1,0:T(8,128)} async-done(((f32[64,5120]{1,0:T(8,128)}), f32[64,1280]{1,0:T(8,128)}) %reduce-scatter.2.cloned.1.call-update) | async-done | bytes 327696 | tf_op jit(solution)/shard_map/reduce_scatter | solution.py:124
  1031.6 1.7 add_convert_fusion.1
  (75 shorter events, 9.1 us)
Async XLA Ops:
  7.2 134.5 %all-gather.4.cloned.1.call-start = ((), (), s32[]{:S(2)}) async-start(), calls=%async_computation.2 | async-start | bytes 26214400 | tf_op jit(solution)/shard_map/all_gather | solution.py:79
  7.9 582.8 %all-gather.6.cloned.1.call-start = ((), (), s32[]{:S(2)}) async-start(), calls=%async_computation.3 | async-start | bytes 23592960 | tf_op jit(solution)/shard_map/all_gather | solution.py:102
  8.6 985.4 %all-gather.8.cloned.1.call-start = ((), (), s32[]{:S(2)}) async-start(), calls=%async_computation.4 | async-start | bytes 23592960 | tf_op jit(solution)/shard_map/all_gather | solution.py:122
  9.4 5.7 copy-start.10
  9.4 132.3 %copy-start.7 = (f32[5120]{0:T(1024)S(1)}, f32[5120]{0:T(1024)}, u32[]{:S(2)}) copy-start(f32[5120]{0:T(1024)} %param.14) | copy-start | bytes 61444
  141.7 20.1 %copy-start.2 = (bf16[640,8,2,256]{3,1,2,0:T(8,128)(2,1)S(1)}, bf16[640,8,2,256]{3,1,2,0:T(8,128)(2,1)}, u32[]{:S(2)}) copy-start(bf16[640,8,2,256]{3,1,2,0:T(8,128)(2,1)} %copy.78) | copy-start | bytes 15728644
  184.2 6.5 copy-start.1
  184.2 6.5 copy-start.8
  210.7 6.2 copy-start.3
  210.7 392.2 %all-to-all-start = ((bf16[8,512,2,256]{3,1,2,0:T(8,128)(2,1)}), bf16[8,512,2,256]{3,1,2,0:T(8,128)(2,1)}, u32[]{:S(2)}, u32[]{:S(2)}) async-start(bf16[8,512,2,256]{3,1,2,0:T(8,128)(2,1)} %broadcast_select_fusion), calls=%async_computation | async-start | bytes 8388608 | tf_op jit(solution)/shard_map/all_to_all | solution.py:92
  216.2 5.4 copy-start.11
  216.3 815.3 %reduce-scatter.2.cloned.1.call-start = ((), (), s32[]{:S(2)}) async-start(), calls=%async_computation.5 | async-start | bytes 1638400 | tf_op jit(solution)/shard_map/reduce_scatter | solution.py:124
  223.8 376.2 %copy-start.9 = (f32[128]{0:T(128)S(1)}, f32[128]{0:T(128)}, u32[]{:S(2)}) copy-start(f32[128]{0:T(128)} %param.15) | copy-start | bytes 1540
  601.0 0.7 copy-start.4
  605.4 3.3 copy-start
  615.6 9.2 copy-start.6
  625.0 9.1 copy-start.5
Sparse Core Ops, SparseCore 0:
  9.6 132.0 all-gather.3
  143.2 447.4 all-gather.5
  592.3 401.7 all-gather.7
  1006.0 25.5 reduce-scatter.1
where the time goes:
time: 1040 us
  waiting for transfers between devices  862 us (83%)
  matrix products  59.5 us (6%)
  other arithmetic  52.7 us (5%)
  local copies, waits for them, and re-layouts  44.9 us (4%)
  between operations  15.5 us (1%)
    all_gather x1, waiting for transfers between devices, local(): lax.all_gather(w_q, 'ctx', axis=0, tiled=True)  367 us
    all_gather x1, waiting for transfers between devices, local(): lax.all_gather(w_o, 'ctx', axis=1, tiled=True)  352 us
    all_gather x1, waiting for transfers between devices, local(): piece = lax.all_gather(prompt_hidden, 'head', axis=2, tiled=True)  126 us
  transfers between devices with their start and end apart: 5, of which 4 were waited for; matrix products, arithmetic and copies ran while one was open for 14% of the time, Pallas kernels for 0%

commit v1 on v0

--- a/solution.py
+++ b/solution.py
@@ -5,6 +5,7 @@
 
 EPS = 1e-06
 THETA = 1000000.0
+CHUNKS = 2
 
 
 def rotary(vector, position):
@@ -74,35 +75,46 @@
     q_local = q_width // head_dim
     group_size = q_local // kv_local
     ctx_index = lax.axis_index("ctx")
-    prompt_rows = prompts * slab
+    ctx_size = lax.axis_size("ctx")
     flat_weights = w_kv.reshape(model_width, 2 * kv_width)
-    piece = lax.all_gather(prompt_hidden, "head", axis=2, tiled=True)
-    count = piece.shape[2]
-    wide_piece = piece.astype(jnp.float32).reshape(prompt_rows, count)
-    scaled_piece = (wide_piece * norm_gain).astype(jnp.bfloat16)
-    running_sum = jnp.dot(scaled_piece, flat_weights, preferred_element_type=jnp.float32)
-    squares = jnp.sum(wide_piece * wide_piece, -1)
-    prefill_inverse = lax.rsqrt(squares / model_width + EPS)[:, None]
-    raw = (running_sum * prefill_inverse).reshape(prompts, slab, 2, kv_local, head_dim)
-    positions = (ctx_index * slab + jnp.arange(slab, dtype=jnp.int32)).astype(jnp.float32)
-    prompt_keys = rotary(head_norm(raw[:, :, 0], k_gain), positions[None, :, None])
-    cache_local = jnp.stack([prompt_keys, raw[:, :, 1]], 2).astype(jnp.bfloat16)
-    cache_local = cache_local.reshape(prompts, slab, 2, kv_width)
-    ordered = jnp.take(cache_local, group_prompt, axis=0)
-    kv_cache = lax.all_to_all(ordered, "ctx", split_axis=0, concat_axis=1, tiled=True)
-    length = jnp.take(prompt_lengths, jnp.take(group_prompt, ctx_index))
     steps = sample_hidden.shape[1]
     samples = sample_hidden.shape[2]
     token_rows = steps * samples
     wide = sample_hidden.reshape(token_rows, model_width).astype(jnp.float32)
     token_inverse = lax.rsqrt(jnp.mean(wide * wide, -1) + EPS)[:, None]
     token_scaled = (wide * norm_gain).astype(jnp.bfloat16)
-    queries = jnp.dot(
-        token_scaled,
-        lax.all_gather(w_q, "ctx", axis=0, tiled=True),
-        preferred_element_type=jnp.float32,
-    )
-    queries = queries * token_inverse
+    row_depth = w_q.shape[0]
+    by_feature = token_scaled.reshape(token_rows, ctx_size, row_depth).transpose(1, 0, 2)
+    all_tokens = lax.all_to_all(by_feature, "ctx", split_axis=0, concat_axis=0, tiled=True)
+    query_part = jnp.dot(
+        all_tokens.reshape(ctx_size * token_rows, row_depth), w_q, preferred_element_type=jnp.float32
+    ).reshape(ctx_size, token_rows, q_width)
+    query_part = lax.all_to_all(query_part, "ctx", split_axis=0, concat_axis=0, tiled=True)
+    queries = jnp.sum(query_part, 0) * token_inverse
+
+    chunk_rows = slab // CHUNKS
+    cache_chunks = []
+    for chunk in range(CHUNKS):
+        hidden = lax.slice_in_dim(prompt_hidden, chunk * chunk_rows, (chunk + 1) * chunk_rows, axis=1)
+        piece = lax.all_gather(hidden, "head", axis=2, tiled=True)
+        wide_piece = piece.astype(jnp.float32).reshape(prompts * chunk_rows, model_width)
+        scaled_piece = (wide_piece * norm_gain).astype(jnp.bfloat16)
+        running_sum = jnp.dot(scaled_piece, flat_weights, preferred_element_type=jnp.float32)
+        squares = jnp.sum(wide_piece * wide_piece, -1)
+        prefill_inverse = lax.rsqrt(squares / model_width + EPS)[:, None]
+        raw = (running_sum * prefill_inverse).reshape(prompts, chunk_rows, 2, kv_local, head_dim)
+        positions = (
+            ctx_index * slab + chunk * chunk_rows + jnp.arange(chunk_rows, dtype=jnp.int32)
+        ).astype(jnp.float32)
+        prompt_keys = rotary(head_norm(raw[:, :, 0], k_gain), positions[None, :, None])
+        cache_local = jnp.stack([prompt_keys, raw[:, :, 1]], 2).astype(jnp.bfloat16)
+        cache_local = cache_local.reshape(prompts, chunk_rows, 2, kv_width)
+        ordered = jnp.take(cache_local, group_prompt, axis=0)
+        cache_chunks.append(
+            lax.all_to_all(ordered, "ctx", split_axis=0, concat_axis=0, tiled=True)
+        )
+    kv_cache = jnp.stack(cache_chunks, 1).reshape(1, ctx_size * slab, 2, kv_width)
+    length = jnp.take(prompt_lengths, jnp.take(group_prompt, ctx_index))
     fresh = jnp.dot(token_scaled, flat_weights, preferred_element_type=jnp.float32) * token_inverse
     fresh = fresh.reshape(token_rows, 2, kv_local, head_dim)
     row_position = jnp.repeat(length + jnp.arange(steps, dtype=jnp.int32), samples).astype(
@@ -118,9 +130,13 @@
     prefix_keys = kv_cache[0, :, 0].reshape(-1, kv_local, head_dim)
     prefix_values = kv_cache[0, :, 1].reshape(-1, kv_local, head_dim)
     attended = attend(queries, prefix_keys, prefix_values, new_keys, new_values, length, samples)
-    partial_out = jnp.dot(
-        attended, lax.all_gather(w_o, "ctx", axis=1, tiled=True), preferred_element_type=jnp.float32
+    all_attended = lax.all_gather(attended, "ctx", axis=0, tiled=True)
+    partial_out = jnp.dot(all_attended, w_o, preferred_element_type=jnp.float32)
+    partial_out = lax.all_to_all(
+        partial_out.reshape(ctx_size, token_rows, w_o.shape[1]),
+        "ctx", split_axis=0, concat_axis=0, tiled=True,
     )
+    partial_out = partial_out.transpose(1, 0, 2).reshape(token_rows, model_width)
     summed = lax.psum_scatter(partial_out, "head", scatter_dimension=1, tiled=True)
     out_width = summed.shape[1]
     residual = lax.dynamic_slice_in_dim(wide, lax.axis_index("head") * out_width, out_width, 1)

time: 1040 us -> 497 us (0.48)
  waiting for transfers between devices: 862 us -> 261 us
  blocking collectives: 0 us -> 34.2 us
  starting transfers between devices: 5.7 us -> 21 us
  matrix products: 59.5 us -> 47.9 us
    all_gather x3, waiting for transfers between devices: 844 us -> 155 us  [the longest x2 106 us: local(): piece = lax.all_gather(hidden, 'head', axis=2, tiled=True)]
    all_to_all x1 -> x4, waiting for transfers between devices: 0.01 us -> 89.7 us  [the longest x2 81.9 us: local(): lax.all_to_all(ordered, 'ctx', split_axis=0, concat_axis=0, tiled=True)]
    all_to_all x0 -> x1, blocking collectives: none -> 34.2 us  [local(): lax.all_to_all(partial_out.reshape(ctx_size, token_rows, w_o.shape[1]), '...]
    all_to_all x1 -> x4, starting transfers between devices: 5.54 us -> 20.9 us  [the longest x2 9.95 us: local(): lax.all_to_all(ordered, 'ctx', split_axis=0, concat_axis=0, tiled=True)]
    dot_general x2, matrix products: 20.7 us -> 7.97 us  [the longest x1 4.16 us: local(): partial_out = jnp.dot(all_attended, w_o, preferred_element_type=jnp.float32)]
    unnamed x28 -> x45, local copies, waits for them, and re-layouts: 17.5 us -> 21.5 us
  transfers between devices with their start and end apart: 5 -> 8, of which waited for: 4 -> 7; matrix products, arithmetic and copies ran while one was open for 14% -> 21% of each run, Pallas kernels for 0% -> 0%
where the time goes in v1:
time: 497 us; the launch traced here: 489 us
  waiting for transfers between devices  261 us (53%)
  other arithmetic  55.7 us (11%)
  local copies, waits for them, and re-layouts  54 us (11%)
  matrix products  47.9 us (10%)
  blocking collectives  34.2 us (7%)
  starting transfers between devices  21 us (4%)
  between operations  16 us (3%)
    all_gather x2, waiting for transfers between devices, local(): piece = lax.all_gather(hidden, 'head', axis=2, tiled=True)  106 us
    all_to_all x2, waiting for transfers between devices, local(): lax.all_to_all(ordered, 'ctx', split_axis=0, concat_axis=0, tiled=True)  81.9 us
    all_gather x1, waiting for transfers between devices, local(): all_attended = lax.all_gather(attended, 'ctx', axis=0, tiled=True)  48.9 us
    all_to_all x1, blocking collectives, local(): lax.all_to_all(partial_out.reshape(ctx_size, token_rows, w_o.shape[1]), '...  34.2 us
    unnamed x45, local copies, waits for them, and re-layouts  21.5 us
    dot_general x2, matrix products, local(): jnp.dot(scaled_piece, flat_weights, preferred_element_type=jnp.float32)  19.4 us
    reduce_scatter x1, waiting for transfers between devices, local(): lax.psum_scatter(partial_out, 'head', scatter_dimension=1, tiled=True)  15.5 us
    reduce_sum x1, other arithmetic, local(): squares = jnp.sum(wide_piece * wide_piece, -1)  14.9 us
  transfers between devices with their start and end apart: 8, of which 7 were waited for; matrix products, arithmetic and copies ran while one was open for 21% of the time, Pallas kernels for 0%

profile of v1, /device:TPU:3, one launch (start us, length us, event | category | flops | bytes accessed | tf_op | source)
XLA Modules:
  0.0 489.5 jit_solution(1599557287418921707)
XLA Ops:
  7.2 5.4 %fusion.24 = (bf16[4,256,1280]{2,1,0:T(8,128)(2,1)}, bf16[4,256,1280]{2,1,0:T(8,128)(2,1)}) fusion(bf16[4,512,1280]{2,1,0:T(8,128)(2,1)} %param.12), kind=kLoop, calls=%fused_computation.103 | loop fusion | bytes 10485760 | tf_op jit(solution)/shard_map/slice | solution.py:98
  18.6 5.6 %all-to-all-start.2 = ((bf16[8,64,640]{2,1,0:T(8,128)(2,1)}), bf16[8,64,640]{2,1,0:T(8,128)(2,1)S(1)}, u32[]{:S(2)}, u32[]{:S(2)}) async-start(bf16[8,64,640]{2,1,0:T(8,128)(2,1)} %fusion.13), calls=%async_computation.2 | async-start | bytes 1310720 | tf_op jit(solution)/shard_map/all_to_all | solution.py:88
  24.2 6.6 %copy.109 = bf16[640,8,2,256]{3,1,2,0:T(8,128)(2,1)} copy(bf16[640,8,2,256]{3,2,1,0:T(2,128)(2,1)} %bitcast.130) | data formatting | bytes 10485760
  32.5 7.8 %all-to-all-done.2 = bf16[8,64,640]{2,1,0:T(8,128)(2,1)S(1)} async-done(((bf16[8,64,640]{2,1,0:T(8,128)(2,1)}), bf16[8,64,640]{2,1,0:T(8,128)(2,1)S(1)}, u32[]{:S(2)}, u32[]{:S(2)}) %all-to-all-start.2) | async-done | bytes 655392 | tf_op jit(solution)/shard_map/all_to_all | solution.py:88
  40.3 3.8 fusion.7
  44.1 5.4 %all-to-all-start.3 = ((f32[8,64,2048]{2,1,0:T(8,128)}), f32[8,64,2048]{2,1,0:T(8,128)}, u32[]{:S(2)}, u32[]{:S(2)}) async-start(f32[8,64,2048]{2,1,0:T(8,128)} %fusion.7), calls=%async_computation.3 | async-start | bytes 8388608 | tf_op jit(solution)/shard_map/all_to_all | solution.py:92
  49.5 34.0 %all-gather.4.cloned.1.call-done = bf16[4,256,5120]{2,1,0:T(8,128)(2,1)} async-done(((bf16[4,256,1280]{2,1,0:T(8,128)(2,1)}), bf16[4,256,5120]{2,1,0:T(8,128)(2,1)}) %all-gather.4.cloned.1.call-update) | async-done | bytes 10485776 | tf_op jit(solution)/shard_map/all_gather | solution.py:99
  83.5 71.8 %all-gather.6.cloned.1.call-done = bf16[4,256,5120]{2,1,0:T(8,128)(2,1)} async-done(((bf16[4,256,1280]{2,1,0:T(8,128)(2,1)}), bf16[4,256,5120]{2,1,0:T(8,128)(2,1)}) %all-gather.6.cloned.1.call-update) | async-done | bytes 10485776 | tf_op jit(solution)/shard_map/all_gather | solution.py:99
  155.3 14.9 %fusion.1 = (f32[4,256]{1,0:T(4,128)S(1)}, bf16[4,256,5120]{2,1,0:T(8,128)(2,1)}, bf16[4,256,5120]{2,1,0:T(8,128)(2,1)S(1)}, f32[4,256]{1,0:T(4,128)S(1)}) fusion(bf16[4,256,5120]{2,1,0:T(8,128)(2,1)} %all-gather.4.cloned.1.call-done, f32[5120]{0:T(1024)S(1)} %copy-done.12, bf16[4,256,5120]{2,1,0:T(8,128)(2,1)} %all-gather.6.cloned.1.call-done), kind=kLoop, calls=%fused_computation.7 | loop fusion | flops 52426752 | bytes 41971712 | tf_op jit(solution)/shard_map/reduce_sum | solution.py:103
  170.2 8.6 %convolution_multiply_fusion = f32[1024,512]{1,0:T(8,128)} fusion(bf16[1024,5120]{1,0:T(8,128)(2,1)S(1)} %bitcast.125, bf16[5120,512]{1,0:T(8,128)(2,1)} %bitcast.121, f32[1024]{0:T(1024)S(1)} %bitcast.144), kind=kOutput, calls=%fused_computation.21 | convolution fusion | flops 5369233408 | bytes 17829888 | tf_op jit(solution)/shard_map/dot_general | solution.py:102
  178.8 2.6 reshape.502
  181.4 10.8 %convolution_multiply_fusion.1 = f32[1024,512]{1,0:T(8,128)} fusion(bf16[1024,5120]{1,0:T(8,128)(2,1)} %bitcast.124, bf16[5120,512]{1,0:T(8,128)(2,1)} %bitcast.122, f32[1024]{0:T(1024)S(1)} %bitcast.143), kind=kOutput, calls=%fused_computation.22 | convolution fusion | flops 5369233408 | bytes 17829888 | tf_op jit(solution)/shard_map/dot_general | solution.py:102
  192.2 3.6 reshape.501
  201.1 3.8 multiply_multiply_fusion.1
  218.6 4.6 broadcast_select_fusion.1
  223.2 5.6 %all-to-all-start = ((bf16[8,256,2,256]{3,1,2,0:T(8,128)(2,1)}), bf16[8,256,2,256]{3,1,2,0:T(8,128)(2,1)S(1)}, u32[]{:S(2)}, u32[]{:S(2)}) async-start(bf16[8,256,2,256]{3,1,2,0:T(8,128)(2,1)} %get-tuple-element.59), calls=%async_computation | async-start | bytes 4194304 | tf_op jit(solution)/shard_map/all_to_all | solution.py:114
  230.7 45.9 %all-to-all-done = bf16[8,256,2,256]{3,1,2,0:T(8,128)(2,1)S(1)} async-done(((bf16[8,256,2,256]{3,1,2,0:T(8,128)(2,1)}), bf16[8,256,2,256]{3,1,2,0:T(8,128)(2,1)S(1)}, u32[]{:S(2)}, u32[]{:S(2)}) %all-to-all-start) | async-done | bytes 2097184 | tf_op jit(solution)/shard_map/all_to_all | solution.py:114
  276.6 4.3 all-to-all-start.1
  281.1 3.5 convolution_multiply_fusion.2
  287.5 2.5 reduce_sum.96
  292.0 36.0 %all-to-all-done.1 = bf16[8,256,2,256]{3,1,2,0:T(8,128)(2,1)} async-done(((bf16[8,256,2,256]{3,1,2,0:T(8,128)(2,1)}), bf16[8,256,2,256]{3,1,2,0:T(8,128)(2,1)}, u32[]{:S(2)}, u32[]{:S(2)}) %all-to-all-start.1) | async-done | bytes 2097184 | tf_op jit(solution)/shard_map/all_to_all | solution.py:114
  330.4 2.4 fusion.25
  333.6 3.1 copy.83
  336.8 8.1 %bitcast_reduce_fusion = (f32[2,8,64]{2,1,0:T(8,128)S(1)}, f32[2,4096,64,8]{1,2,3,0:T(8,128)}) fusion(pred[4096]{0:T(1024)(128)(4,1)S(1)} %iota_compare_fusion, bf16[4096,2,128,1]{0,2,3,1:T(8,128)(2,1)S(1)} %bitcast.126, bf16[64,2,8,128]{3,0,2,1:T(8,128)(2,1)S(1)} %fusion.14), kind=kOutput, calls=%fused_computation.11 | convolution fusion | flops 1082129408 | bytes 19144704 | tf_op jit(solution)/shard_map/rkgd,lkd->kgrl/dot_general | solution.py:28
  345.0 9.1 %fusion.5 = f32[2,8,64]{2,1,0:T(8,128)S(1)} fusion(f32[2,4096,64,8]{1,2,3,0:T(8,128)} %get-tuple-element.66, f32[2,8,64]{2,1,0:T(8,128)S(1)} %max.8, pred[4096]{0:T(1024)(128)(4,1)S(1)} %iota_compare_fusion), kind=kLoop, calls=%fused_computation.14 | loop fusion | flops 12581888 | bytes 16789504 | tf_op jit(solution)/shard_map/reduce_sum | solution.py:45
  354.1 2.9 copy.82
  356.9 8.2 %fusion.6 = f32[2,128,8,64]{1,3,2,0:T(8,128)S(1)} fusion(bf16[4096,2,128,1]{0,2,3,1:T(8,128)(2,1)} %bitcast.136, f32[2,4096,64,8]{1,2,3,0:T(8,128)} %get-tuple-element.66, f32[2,8,64]{2,1,0:T(8,128)S(1)} %add.194, f32[2,8,64]{2,1,0:T(8,128)S(1)} %max.8, pred[4096]{0:T(1024)(128)(4,1)S(1)} %iota_compare_fusion), kind=kOutput, calls=%fused_computation.15 | convolution fusion | flops 1090519040 | bytes 19410944 | tf_op jit(solution)/shard_map/kgrl,lkd->rkgd/dot_general | solution.py:48
  366.5 48.9 %all-gather.8.cloned.1.call-done = bf16[512,2048]{1,0:T(8,128)(2,1)} async-done(((bf16[64,2048]{1,0:T(8,128)(2,1)}), bf16[512,2048]{1,0:T(8,128)(2,1)}) %all-gather.8.cloned.1.call-update) | async-done | bytes 2097168 | tf_op jit(solution)/shard_map/all_gather | solution.py:133
  415.3 4.2 fusion.27
  419.5 34.2 %all_to_all.25 = f32[8,64,640]{2,1,0:T(8,128)S(1)} all-to-all(f32[8,64,640]{2,1,0:T(8,128)S(1)} %bitcast.139), channel_id=1, replica_groups=mesh['ctx'=8,'head'=4] {'ctx'}, dimensions={0} | all-to-all | bytes 2621440 | tf_op jit(solution)/shard_map/all_to_all | solution.py:135
  454.9 10.3 %copy.94 = bf16[1,4096,2,256]{3,2,1,0:T(2,128)(2,1)} copy(bf16[1,4096,2,256]{3,1,2,0:T(8,128)(2,1)} %bitcast.120) | data formatting | bytes 8388608
  465.2 15.5 %reduce-scatter.2.cloned.1.call-done = f32[64,1280]{1,0:T(8,128)} async-done(((f32[64,5120]{1,0:T(8,128)}), f32[64,1280]{1,0:T(8,128)}) %reduce-scatter.2.cloned.1.call-update) | async-done | bytes 327696 | tf_op jit(solution)/shard_map/reduce_scatter | solution.py:140
  (118 shorter events, 39.5 us)
Async XLA Ops:
  7.2 33.1 %copy-start = (bf16[640,2048]{1,0:T(8,128)(2,1)S(1)}, bf16[640,2048]{1,0:T(8,128)(2,1)}, u32[]{:S(2)}) copy-start(bf16[640,2048]{1,0:T(8,128)(2,1)} %param.19) | copy-start | bytes 7864324
  7.2 76.3 %all-gather.4.cloned.1.call-start = ((), (), s32[]{:S(2)}) async-start(), calls=%async_computation.6 | async-start | bytes 13107200 | tf_op jit(solution)/shard_map/all_gather | solution.py:99
  12.6 1.1 copy-start.7
  12.6 142.6 %all-gather.6.cloned.1.call-start = ((), (), s32[]{:S(2)}) async-start(), calls=%async_computation.7 | async-start | bytes 13107200 | tf_op jit(solution)/shard_map/all_gather | solution.py:99
  13.7 2.5 copy-start.11
  13.8 1.1 copy-start.6
  18.6 21.7 %all-to-all-start.2 = ((bf16[8,64,640]{2,1,0:T(8,128)(2,1)}), bf16[8,64,640]{2,1,0:T(8,128)(2,1)S(1)}, u32[]{:S(2)}, u32[]{:S(2)}) async-start(bf16[8,64,640]{2,1,0:T(8,128)(2,1)} %fusion.13), calls=%async_computation.2 | async-start | bytes 1310720 | tf_op jit(solution)/shard_map/all_to_all | solution.py:88
  24.2 6.7 %copy-start.16 = (s32[8]{0:T(128)S(1)}, s32[8]{0:T(128)}, u32[]{:S(2)}) copy-start(s32[8]{0:T(128)} %param.14) | copy-start | bytes 100
  44.1 111.2 %copy-start.12 = (f32[5120]{0:T(1024)S(1)}, f32[5120]{0:T(1024)}, u32[]{:S(2)}) copy-start(f32[5120]{0:T(1024)} %param.16) | copy-start | bytes 61444
  44.1 179.1 %all-to-all-start.3 = ((f32[8,64,2048]{2,1,0:T(8,128)}), f32[8,64,2048]{2,1,0:T(8,128)}, u32[]{:S(2)}, u32[]{:S(2)}) async-start(f32[8,64,2048]{2,1,0:T(8,128)} %fusion.7), calls=%async_computation.3 | async-start | bytes 8388608 | tf_op jit(solution)/shard_map/all_to_all | solution.py:92
  195.8 3.9 copy-start.3
  198.5 2.5 copy-start.14
  201.1 3.8 copy-start.9
  201.1 3.8 copy-start.10
  204.9 3.6 copy-start.8
  206.7 2.9 copy-start.4
  223.2 5.6 %copy-start.17 = (s32[8]{0:T(128)S(1)}, s32[8]{0:T(128)}, u32[]{:S(2)}) copy-start(s32[8]{0:T(128)} %param.14) | copy-start | bytes 100
  223.2 6.2 %copy-start.13 = (f32[5120]{0:T(1024)S(1)}, f32[5120]{0:T(1024)}, u32[]{:S(2)}) copy-start(f32[5120]{0:T(1024)} %param.16) | copy-start | bytes 61444
  223.2 53.4 %all-to-all-start = ((bf16[8,256,2,256]{3,1,2,0:T(8,128)(2,1)}), bf16[8,256,2,256]{3,1,2,0:T(8,128)(2,1)S(1)}, u32[]{:S(2)}, u32[]{:S(2)}) async-start(bf16[8,256,2,256]{3,1,2,0:T(8,128)(2,1)} %get-tuple-element.59), calls=%async_computation | async-start | bytes 4194304 | tf_op jit(solution)/shard_map/all_to_all | solution.py:114
  276.6 51.3 %all-to-all-start.1 = ((bf16[8,256,2,256]{3,1,2,0:T(8,128)(2,1)}), bf16[8,256,2,256]{3,1,2,0:T(8,128)(2,1)}, u32[]{:S(2)}, u32[]{:S(2)}) async-start(bf16[8,256,2,256]{3,1,2,0:T(8,128)(2,1)} %get-tuple-element.60), calls=%async_computation.1 | async-start | bytes 4194304 | tf_op jit(solution)/shard_map/all_to_all | solution.py:114
  281.0 134.4 %all-gather.8.cloned.1.call-start = ((), (), s32[]{:S(2)}) async-start(), calls=%async_computation.8 | async-start | bytes 2359296 | tf_op jit(solution)/shard_map/all_gather | solution.py:133
  281.1 4.3 copy-start.18
  287.5 3.0 copy-start.15
  330.4 3.2 copy-start.2
  345.0 9.1 %copy-start.5 = (bf16[1,4096,1,256]{3,1,2,0:T(8,128)(2,1)S(1)}, bf16[1,4096,1,256]{3,1,2,0:T(8,128)(2,1)}, u32[]{:S(2)}) copy-start(bf16[1,4096,1,256]{3,1,2,0:T(8,128)(2,1)} %get-tuple-element.42) | copy-start | bytes 6291460
  366.4 114.3 %reduce-scatter.2.cloned.1.call-start = ((), (), s32[]{:S(2)}) async-start(), calls=%async_computation.9 | async-start | bytes 1638400 | tf_op jit(solution)/shard_map/reduce_scatter | solution.py:140
  454.9 27.6 %copy-start.1 = (bf16[640,2048]{1,0:T(8,128)(2,1)S(1)}, bf16[640,2048]{1,0:T(8,128)(2,1)}, u32[]{:S(2)}) copy-start(bf16[640,2048]{1,0:T(8,128)(2,1)} %param.19) | copy-start | bytes 7864324
Sparse Core Ops, SparseCore 0:
  12.7 70.6 all-gather.3
  85.0 70.1 all-gather.5
  366.5 48.7 all-gather.7
  455.0 25.6 reduce-scatter.1

commit v2 on v1

--- a/solution.py
+++ b/solution.py
@@ -1,6 +1,10 @@
+import functools
+
 import jax
 import jax.numpy as jnp
 from jax import lax
+from jax.experimental import pallas as pl
+from jax.experimental.pallas import tpu as pltpu
 from jax.sharding import PartitionSpec as P
 
 EPS = 1e-06
@@ -52,6 +56,150 @@
         "kgru,ukd->rkgd", suffix_weight, new_values, preferred_element_type=jnp.float32
     )
     return result.reshape(total_rows, -1).astype(jnp.bfloat16)
+
+
+def project_kernel(
+    ctx_size, head_size, attended_ref, w_ref, out_ref,
+    gathered, partial, landed, gather_send, gather_recv, part_send, part_recv, own_sem,
+):
+    ctx = lax.axis_index("ctx")
+    head = lax.axis_index("head")
+    per = ctx_size // head_size
+    owner = ctx // per
+    rank = ctx % per
+    is_owner = owner == head
+    mesh_id = pl.DeviceIdType.MESH
+
+    barrier = pltpu.get_barrier_semaphore()
+    for k in range(1, ctx_size):
+        source = lax.rem(ctx - k + ctx_size, ctx_size)
+        pl.semaphore_signal(barrier, inc=1, device_id=(source, head), device_id_type=mesh_id)
+    for h in range(head_size):
+        for r in range(per):
+            source = head * per + r
+
+            @pl.when(jnp.logical_or(source != ctx, h != head))
+            def _():
+                pl.semaphore_signal(barrier, inc=1, device_id=(source, h), device_id_type=mesh_id)
+
+    @pl.when(is_owner)
+    def _():
+        pl.semaphore_wait(barrier, 2 * ctx_size - 2)
+
+    @pl.when(jnp.logical_not(is_owner))
+    def _():
+        pl.semaphore_wait(barrier, 2 * ctx_size - 1)
+
+    def gather_copy(k):
+        target = lax.rem(ctx + k, ctx_size)
+        return pltpu.make_async_remote_copy(
+            src_ref=attended_ref, dst_ref=gathered.at[k],
+            send_sem=gather_send.at[k], recv_sem=gather_recv.at[k],
+            device_id=(target, head), device_id_type=mesh_id,
+        )
+
+    def part_copy(k):
+        target = lax.rem(ctx - k + ctx_size, ctx_size)
+        slot = head * per + rank
+        return pltpu.make_async_remote_copy(
+            src_ref=partial.at[k], dst_ref=landed.at[slot],
+            send_sem=part_send.at[k], recv_sem=part_recv.at[slot],
+            device_id=(target, owner), device_id_type=mesh_id,
+        )
+
+    def own_copy():
+        return pltpu.make_async_copy(partial.at[0], landed.at[head * per + rank], own_sem)
+
+    for k in range(1, ctx_size):
+        gather_copy(k).start()
+    gathered[0] = attended_ref[...]
+    rows, depth = attended_ref.shape
+    width = w_ref.shape[1]
+    half = ctx_size // 2
+    for part in range(2):
+        first = part * half
+        for k in range(max(first, 1), first + half):
+            gather_copy(k).wait_recv()
+        block = gathered[first : first + half].reshape(half * rows, depth)
+        product = jnp.dot(block, w_ref[...], preferred_element_type=jnp.float32)
+        partial[first : first + half] = product.reshape(half, rows, width)
+        for k in range(first, first + half):
+            if k:
+                part_copy(k).start()
+            else:
+
+                @pl.when(is_owner)
+                def _():
+                    own_copy().start()
+
+                @pl.when(jnp.logical_not(is_owner))
+                def _():
+                    part_copy(0).start()
+
+    for k in range(1, ctx_size):
+        gather_copy(k).wait_send()
+    for r in range(per):
+        source = head * per + r
+        for h in range(head_size):
+            mine = jnp.logical_and(source == ctx, h == head)
+            slot = h * per + r
+
+            @pl.when(mine)
+            def _():
+                own_copy().wait()
+
+            @pl.when(jnp.logical_not(mine))
+            def _():
+                pltpu.make_async_remote_copy(
+                    src_ref=partial.at[0], dst_ref=landed.at[slot],
+                    send_sem=part_send.at[0], recv_sem=part_recv.at[slot],
+                    device_id=(source, h), device_id_type=mesh_id,
+                ).wait_recv()
+
+        total = landed[r]
+        for h in range(1, head_size):
+            total = total + landed[h * per + r]
+        out_ref[:, r * width : (r + 1) * width] = total
+    for k in range(ctx_size):
+        if k:
+            part_copy(k).wait_send()
+        else:
+
+            @pl.when(jnp.logical_not(is_owner))
+            def _():
+                part_copy(0).wait_send()
+
+
+def project(attended, w_o):
+    ctx_size = lax.axis_size("ctx")
+    head_size = lax.axis_size("head")
+    per = ctx_size // head_size
+    rows, depth = attended.shape
+    width = w_o.shape[1]
+    return pl.pallas_call(
+        functools.partial(project_kernel, ctx_size, head_size),
+        out_shape=jax.ShapeDtypeStruct((rows, per * width), jnp.float32),
+        in_specs=[pl.BlockSpec(memory_space=pltpu.VMEM)] * 2,
+        out_specs=pl.BlockSpec(memory_space=pltpu.VMEM),
+        scratch_shapes=[
+            pltpu.VMEM((ctx_size, rows, depth), jnp.bfloat16),
+            pltpu.VMEM((ctx_size, rows, width), jnp.float32),
+            pltpu.VMEM((head_size * per, rows, width), jnp.float32),
+            pltpu.SemaphoreType.DMA((ctx_size,)),
+            pltpu.SemaphoreType.DMA((ctx_size,)),
+            pltpu.SemaphoreType.DMA((ctx_size,)),
+            pltpu.SemaphoreType.DMA((head_size * per,)),
+            pltpu.SemaphoreType.DMA,
+        ],
+        compiler_params=pltpu.CompilerParams(
+            collective_id=0, has_side_effects=True, vmem_limit_bytes=32 * 1024 * 1024
+        ),
+        cost_estimate=pl.CostEstimate(
+            flops=2 * ctx_size * rows * depth * width,
+            bytes_accessed=2 * (depth * width + ctx_size * rows * depth),
+            transcendentals=0,
+        ),
+    )(attended, w_o)
 
 
 def local(
@@ -93,10 +241,16 @@
     queries = jnp.sum(query_part, 0) * token_inverse
 
     chunk_rows = slab // CHUNKS
+    exchange = functools.partial(
+        lax.all_to_all, axis_name="ctx", split_axis=0, concat_axis=0, tiled=True
+    )
     cache_chunks = []
     for chunk in range(CHUNKS):
         hidden = lax.slice_in_dim(prompt_hidden, chunk * chunk_rows, (chunk + 1) * chunk_rows, axis=1)
         piece = lax.all_gather(hidden, "head", axis=2, tiled=True)
+        if cache_chunks:
+            piece, ordered = lax.optimization_barrier((piece, ordered))
+            cache_chunks[-1] = exchange(ordered)
         wide_piece = piece.astype(jnp.float32).reshape(prompts * chunk_rows, model_width)
         scaled_piece = (wide_piece * norm_gain).astype(jnp.bfloat16)
         running_sum = jnp.dot(scaled_piece, flat_weights, preferred_element_type=jnp.float32)
@@ -110,9 +264,8 @@
         cache_local = jnp.stack([prompt_keys, raw[:, :, 1]], 2).astype(jnp.bfloat16)
         cache_local = cache_local.reshape(prompts, chunk_rows, 2, kv_width)
         ordered = jnp.take(cache_local, group_prompt, axis=0)
-        cache_chunks.append(
-            lax.all_to_all(ordered, "ctx", split_axis=0, concat_axis=0, tiled=True)
-        )
+        cache_chunks.append(None)
+    cache_chunks[-1] = exchange(ordered)
     kv_cache = jnp.stack(cache_chunks, 1).reshape(1, ctx_size * slab, 2, kv_width)
     length = jnp.take(prompt_lengths, jnp.take(group_prompt, ctx_index))
     fresh = jnp.dot(token_scaled, flat_weights, preferred_element_type=jnp.float32) * token_inverse
@@ -130,14 +283,7 @@
     prefix_keys = kv_cache[0, :, 0].reshape(-1, kv_local, head_dim)
     prefix_values = kv_cache[0, :, 1].reshape(-1, kv_local, head_dim)
     attended = attend(queries, prefix_keys, prefix_values, new_keys, new_values, length, samples)
-    all_attended = lax.all_gather(attended, "ctx", axis=0, tiled=True)
-    partial_out = jnp.dot(all_attended, w_o, preferred_element_type=jnp.float32)
-    partial_out = lax.all_to_all(
-        partial_out.reshape(ctx_size, token_rows, w_o.shape[1]),
-        "ctx", split_axis=0, concat_axis=0, tiled=True,
-    )
-    partial_out = partial_out.transpose(1, 0, 2).reshape(token_rows, model_width)
-    summed = lax.psum_scatter(partial_out, "head", scatter_dimension=1, tiled=True)
+    summed = project(attended, w_o)
     out_width = summed.shape[1]
     residual = lax.dynamic_slice_in_dim(wide, lax.axis_index("head") * out_width, out_width, 1)
     decoded = (residual + summed).astype(jnp.bfloat16).reshape(1, steps, samples, out_width)

time: 497 us -> 455 us (0.915)
  waiting for transfers between devices: 261 us -> 165 us
  Pallas kernels: 0 us -> 88.1 us
  blocking collectives: 34.2 us -> 0 us
  local copies, waits for them, and re-layouts: 54 us -> 63.7 us
  matrix products: 47.9 us -> 41.7 us
    pallas_call x0 -> x1, Pallas kernels: none -> 88.1 us  [project(): pl.pallas_call(functools.partial(project_kernel, ctx_size, head_size), ou...]
    all_gather x1 -> x0, waiting for transfers between devices: 48.9 us -> none  [local(): all_attended = lax.all_gather(attended, 'ctx', axis=0, tiled=True)]
    all_to_all x1 -> x0, blocking collectives: 34.2 us -> none  [local(): lax.all_to_all(partial_out.reshape(ctx_size, token_rows, w_o.shape[1]), '...]
    all_gather x2, waiting for transfers between devices: 106 us -> 75.4 us  [local(): piece = lax.all_gather(hidden, 'head', axis=2, tiled=True)]
    reduce_scatter x1 -> x0, waiting for transfers between devices: 15.5 us -> none  [local(): lax.psum_scatter(partial_out, 'head', scatter_dimension=1, tiled=True)]
    unnamed x45, local copies, waits for them, and re-layouts: 21.5 us -> 36.7 us
    reduce_sum x1 -> x2, other arithmetic: 14.9 us -> 13.7 us  [local(): squares = jnp.sum(wide_piece * wide_piece, -1)]
  transfers between devices with their start and end apart: 8 -> 6, of which waited for: 7 -> 5; matrix products, arithmetic and copies ran while one was open for 21% -> 20% of each run, Pallas kernels for 0% -> 0%
where the time goes in v2:
time: 455 us; the launch traced here: 450 us
  waiting for transfers between devices  165 us (36%)
  Pallas kernels  88.1 us (19%)
  local copies, waits for them, and re-layouts  63.7 us (14%)
  other arithmetic  53.9 us (12%)
  matrix products  41.7 us (9%)
  starting transfers between devices  21.4 us (5%)
  between operations  16.3 us (4%)
    pallas_call x1, Pallas kernels, project(): pl.pallas_call(functools.partial(project_kernel, ctx_size, head_size), ou...  88.1 us
    all_to_all x2, waiting for transfers between devices, local(): cache_chunks[-1] = exchange(ordered)  81.2 us
    all_gather x2, waiting for transfers between devices, local(): piece = lax.all_gather(hidden, 'head', axis=2, tiled=True)  75.4 us
    unnamed x45, local copies, waits for them, and re-layouts  36.7 us
    dot_general x2, matrix products, local(): jnp.dot(scaled_piece, flat_weights, preferred_element_type=jnp.float32)  17.1 us
    reduce_sum x2, other arithmetic, local(): squares = jnp.sum(wide_piece * wide_piece, -1)  13.7 us
    all_to_all x2, starting transfers between devices, local(): cache_chunks[-1] = exchange(ordered)  10 us
  transfers between devices with their start and end apart: 6, of which 5 were waited for; matrix products, arithmetic and copies ran while one was open for 20% of the time, Pallas kernels for 0%

profile of v2, /device:TPU:3, one launch (start us, length us, event | category | flops | bytes accessed | tf_op | source)
XLA Modules:
  0.0 450.2 jit_solution(14094169577254194226)
XLA Ops:
  7.2 5.3 %fusion.24 = (bf16[4,256,1280]{2,1,0:T(8,128)(2,1)}, bf16[4,256,1280]{2,1,0:T(8,128)(2,1)}) fusion(bf16[4,512,1280]{2,1,0:T(8,128)(2,1)} %param.12), kind=kLoop, calls=%fused_computation.103 | loop fusion | bytes 10485760 | tf_op jit(solution)/shard_map/slice | solution.py:249
  16.1 2.4 fusion.13
  18.5 5.6 %all-to-all-start.2 = ((bf16[8,64,640]{2,1,0:T(8,128)(2,1)}), bf16[8,64,640]{2,1,0:T(8,128)(2,1)S(1)}, u32[]{:S(2)}, u32[]{:S(2)}) async-start(bf16[8,64,640]{2,1,0:T(8,128)(2,1)} %fusion.13), calls=%async_computation.2 | async-start | bytes 1310720 | tf_op jit(solution)/shard_map/all_to_all | solution.py:236
  24.0 6.6 %copy.90 = bf16[640,8,2,256]{3,1,2,0:T(8,128)(2,1)} copy(bf16[640,8,2,256]{3,2,1,0:T(2,128)(2,1)} %bitcast.125) | data formatting | bytes 10485760
  32.3 7.8 %all-to-all-done.2 = bf16[8,64,640]{2,1,0:T(8,128)(2,1)S(1)} async-done(((bf16[8,64,640]{2,1,0:T(8,128)(2,1)}), bf16[8,64,640]{2,1,0:T(8,128)(2,1)S(1)}, u32[]{:S(2)}, u32[]{:S(2)}) %all-to-all-start.2) | async-done | bytes 655392 | tf_op jit(solution)/shard_map/all_to_all | solution.py:236
  40.1 3.8 fusion.7
  43.9 5.7 %all-to-all-start.3 = ((f32[8,64,2048]{2,1,0:T(8,128)}), f32[8,64,2048]{2,1,0:T(8,128)}, u32[]{:S(2)}, u32[]{:S(2)}) async-start(f32[8,64,2048]{2,1,0:T(8,128)} %fusion.7), calls=%async_computation.3 | async-start | bytes 8388608 | tf_op jit(solution)/shard_map/all_to_all | solution.py:240
  49.7 33.8 %all-gather.5.cloned.1.call-done = bf16[4,256,5120]{2,1,0:T(8,128)(2,1)} async-done(((bf16[4,256,1280]{2,1,0:T(8,128)(2,1)}), bf16[4,256,5120]{2,1,0:T(8,128)(2,1)}) %all-gather.5.cloned.1.call-update) | async-done | bytes 10485776 | tf_op jit(solution)/shard_map/all_gather | solution.py:250
  83.4 6.9 %fusion.1 = (f32[4,256]{1,0:T(4,128)S(1)}, bf16[4,256,5120]{2,1,0:T(8,128)(2,1)S(1)}) fusion(bf16[4,256,5120]{2,1,0:T(8,128)(2,1)} %all-gather.5.cloned.1.call-done, f32[5120]{0:T(1024)S(1)} %copy-done.11), kind=kLoop, calls=%fused_computation.7 | loop fusion | flops 26213376 | bytes 20996096 | tf_op jit(solution)/shard_map/reduce_sum | solution.py:257
  90.4 8.5 %convolution_multiply_fusion.1 = f32[1024,512]{1,0:T(8,128)} fusion(bf16[1024,5120]{1,0:T(8,128)(2,1)S(1)} %bitcast.119, bf16[5120,512]{1,0:T(8,128)(2,1)} %bitcast.116, f32[1024]{0:T(1024)S(1)} %bitcast.134), kind=kOutput, calls=%fused_computation.22 | convolution fusion | flops 5369233408 | bytes 17829888 | tf_op jit(solution)/shard_map/dot_general | solution.py:256
  98.9 2.7 reshape.495
  108.4 2.0 gather_fusion
  110.4 3.2 broadcast_select_fusion.1
  113.6 41.6 %all-gather.3.cloned.1.call-done = bf16[4,256,5120]{2,1,0:T(8,128)(2,1)} async-done(((bf16[4,256,1280]{2,1,0:T(8,128)(2,1)}), bf16[4,256,5120]{2,1,0:T(8,128)(2,1)}) %all-gather.3.cloned.1.call-update) | async-done | bytes 10485776 | tf_op jit(solution)/shard_map/all_gather | solution.py:250
  155.2 6.9 %fusion.3 = (f32[4,256]{1,0:T(4,128)S(1)}, bf16[4,256,5120]{2,1,0:T(8,128)(2,1)S(1)}) fusion(bf16[4,256,5120]{2,1,0:T(8,128)(2,1)} %all-gather.3.cloned.1.call-done, f32[5120]{0:T(1024)S(1)} %copy-done.12), kind=kLoop, calls=%fused_computation.9 | loop fusion | flops 26213376 | bytes 20996096 | tf_op jit(solution)/shard_map/reduce_sum | solution.py:257
  162.1 8.6 %convolution_multiply_fusion = f32[1024,512]{1,0:T(8,128)} fusion(bf16[1024,5120]{1,0:T(8,128)(2,1)S(1)} %bitcast.120, bf16[5120,512]{1,0:T(8,128)(2,1)} %bitcast.117, f32[1024]{0:T(1024)S(1)} %bitcast.135), kind=kOutput, calls=%fused_computation.21 | convolution fusion | flops 5369233408 | bytes 17829888 | tf_op jit(solution)/shard_map/dot_general | solution.py:256
  170.7 2.7 reshape.496
  180.3 2.0 gather_fusion.1
  182.3 3.2 broadcast_select_fusion
  185.5 5.5 %all-to-all-start.1 = ((bf16[8,256,2,256]{3,1,2,0:T(8,128)(2,1)}), bf16[8,256,2,256]{3,1,2,0:T(8,128)(2,1)S(1)}, u32[]{:S(2)}, u32[]{:S(2)}) async-start(bf16[8,256,2,256]{3,1,2,0:T(8,128)(2,1)} %broadcast_select_fusion), calls=%async_computation.1 | async-start | bytes 4194304 | tf_op jit(solution)/shard_map/all_to_all | solution.py:268
  192.9 45.9 %all-to-all-done.1 = bf16[8,256,2,256]{3,1,2,0:T(8,128)(2,1)S(1)} async-done(((bf16[8,256,2,256]{3,1,2,0:T(8,128)(2,1)}), bf16[8,256,2,256]{3,1,2,0:T(8,128)(2,1)S(1)}, u32[]{:S(2)}, u32[]{:S(2)}) %all-to-all-start.1) | async-done | bytes 2097184 | tf_op jit(solution)/shard_map/all_to_all | solution.py:268
  238.8 4.6 %all-to-all-start = ((bf16[8,256,2,256]{3,1,2,0:T(8,128)(2,1)}), bf16[8,256,2,256]{3,1,2,0:T(8,128)(2,1)}, u32[]{:S(2)}, u32[]{:S(2)}) async-start(bf16[8,256,2,256]{3,1,2,0:T(8,128)(2,1)} %broadcast_select_fusion.1), calls=%async_computation | async-start | bytes 4194304 | tf_op jit(solution)/shard_map/all_to_all | solution.py:253
  243.5 3.5 convolution_multiply_fusion.2
  249.8 2.5 reduce_sum.96
  255.1 35.2 %all-to-all-done = bf16[8,256,2,256]{3,1,2,0:T(8,128)(2,1)} async-done(((bf16[8,256,2,256]{3,1,2,0:T(8,128)(2,1)}), bf16[8,256,2,256]{3,1,2,0:T(8,128)(2,1)}, u32[]{:S(2)}, u32[]{:S(2)}) %all-to-all-start) | async-done | bytes 2097184 | tf_op jit(solution)/shard_map/all_to_all | solution.py:253
  294.3 27.1 %copy.76 = bf16[1,4096,2,256]{3,2,1,0:T(2,128)(2,1)} copy(bf16[1,4096,2,256]{3,1,2,0:T(8,128)(2,1)S(1)} %bitcast.115) | data formatting | bytes 8388608
  321.5 2.9 copy.65
  324.4 3.2 copy.66
  327.6 8.1 %bitcast_reduce_fusion = (f32[2,8,64]{2,1,0:T(8,128)S(1)}, f32[2,4096,64,8]{1,2,3,0:T(8,128)}) fusion(pred[4096]{0:T(1024)(128)(4,1)S(1)} %iota_compare_fusion, bf16[4096,2,128,1]{0,2,3,1:T(8,128)(2,1)S(1)} %bitcast.121, bf16[64,2,8,128]{3,0,2,1:T(8,128)(2,1)S(1)} %fusion.14), kind=kOutput, calls=%fused_computation.11 | convolution fusion | flops 1082129408 | bytes 19144704 | tf_op jit(solution)/shard_map/rkgd,lkd->kgrl/dot_general | solution.py:32
  335.7 9.1 %fusion.5 = f32[2,8,64]{2,1,0:T(8,128)S(1)} fusion(f32[2,4096,64,8]{1,2,3,0:T(8,128)} %get-tuple-element.64, f32[2,8,64]{2,1,0:T(8,128)S(1)} %max.8, pred[4096]{0:T(1024)(128)(4,1)S(1)} %iota_compare_fusion), kind=kLoop, calls=%fused_computation.14 | loop fusion | flops 12581888 | bytes 16789504 | tf_op jit(solution)/shard_map/reduce_sum | solution.py:49
  344.9 7.7 %fusion.6 = f32[2,128,8,64]{1,3,2,0:T(8,128)S(1)} fusion(bf16[4096,2,128,1]{0,2,3,1:T(8,128)(2,1)S(1)} %bitcast.129, f32[2,4096,64,8]{1,2,3,0:T(8,128)} %get-tuple-element.64, f32[2,8,64]{2,1,0:T(8,128)S(1)} %add.192, f32[2,8,64]{2,1,0:T(8,128)S(1)} %max.8, pred[4096]{0:T(1024)(128)(4,1)S(1)} %iota_compare_fusion), kind=kOutput, calls=%fused_computation.15 | convolution fusion | flops 1090519040 | bytes 19410944 | tf_op jit(solution)/shard_map/kgrl,lkd->rkgd/dot_general | solution.py:52
  353.3 88.1 %shard_map.113 = f32[64,1280]{1,0:T(8,128)S(1)} custom-call(bf16[64,2048]{1,0:T(8,128)(2,1)S(1)} %bitcast.113, bf16[2048,640]{1,0:T(8,128)(2,1)S(1)} %copy-done.2), custom_call_target="tpu_custom_call" | custom-call | flops 1342177280 | bytes 4718592 | tf_op jit(solution)/shard_map/pallas_call | solution.py:179
  (113 shorter events, 31.2 us)
Async XLA Ops:
  7.2 33.0 %copy-start = (bf16[640,2048]{1,0:T(8,128)(2,1)S(1)}, bf16[640,2048]{1,0:T(8,128)(2,1)}, u32[]{:S(2)}) copy-start(bf16[640,2048]{1,0:T(8,128)(2,1)} %param.19) | copy-start | bytes 7864324
  7.2 76.3 %all-gather.5.cloned.1.call-start = ((), (), s32[]{:S(2)}) async-start(), calls=%async_computation.5 | async-start | bytes 13107200 | tf_op jit(solution)/shard_map/all_gather | solution.py:250
  12.6 1.1 copy-start.4
  12.6 3.5 copy-start.10
  12.6 142.6 %all-gather.3.cloned.1.call-start = ((), (), s32[]{:S(2)}) async-start(), calls=%async_computation.4 | async-start | bytes 13107200 | tf_op jit(solution)/shard_map/all_gather | solution.py:250
  13.7 1.1 copy-start.3
  18.5 21.7 %all-to-all-start.2 = ((bf16[8,64,640]{2,1,0:T(8,128)(2,1)}), bf16[8,64,640]{2,1,0:T(8,128)(2,1)S(1)}, u32[]{:S(2)}, u32[]{:S(2)}) async-start(bf16[8,64,640]{2,1,0:T(8,128)(2,1)} %fusion.13), calls=%async_computation.2 | async-start | bytes 1310720 | tf_op jit(solution)/shard_map/all_to_all | solution.py:236
  24.0 6.7 %copy-start.16 = (s32[8]{0:T(128)S(1)}, s32[8]{0:T(128)}, u32[]{:S(2)}) copy-start(s32[8]{0:T(128)} %param.14) | copy-start | bytes 100
  43.9 39.5 %copy-start.11 = (f32[5120]{0:T(1024)S(1)}, f32[5120]{0:T(1024)}, u32[]{:S(2)}) copy-start(f32[5120]{0:T(1024)} %param.16) | copy-start | bytes 61444
  43.9 141.6 %all-to-all-start.3 = ((f32[8,64,2048]{2,1,0:T(8,128)}), f32[8,64,2048]{2,1,0:T(8,128)}, u32[]{:S(2)}, u32[]{:S(2)}) async-start(f32[8,64,2048]{2,1,0:T(8,128)} %fusion.7), calls=%async_computation.3 | async-start | bytes 8388608 | tf_op jit(solution)/shard_map/all_to_all | solution.py:240
  98.9 4.7 %copy-start.14 = (f32[128]{0:T(128)S(1)}, f32[128]{0:T(128)}, u32[]{:S(2)}) copy-start(f32[128]{0:T(128)} %param.18) | copy-start | bytes 1540
  101.5 3.3 copy-start.8
  102.3 2.6 copy-start.9
  108.4 46.8 %copy-start.12 = (f32[5120]{0:T(1024)S(1)}, f32[5120]{0:T(1024)}, u32[]{:S(2)}) copy-start(f32[5120]{0:T(1024)} %param.16) | copy-start | bytes 61444
  182.3 8.7 %copy-start.17 = (s32[8]{0:T(128)S(1)}, s32[8]{0:T(128)}, u32[]{:S(2)}) copy-start(s32[8]{0:T(128)} %param.14) | copy-start | bytes 100
  182.3 9.3 %copy-start.13 = (f32[5120]{0:T(1024)S(1)}, f32[5120]{0:T(1024)}, u32[]{:S(2)}) copy-start(f32[5120]{0:T(1024)} %param.16) | copy-start | bytes 61444
  185.5 53.3 %all-to-all-start.1 = ((bf16[8,256,2,256]{3,1,2,0:T(8,128)(2,1)}), bf16[8,256,2,256]{3,1,2,0:T(8,128)(2,1)S(1)}, u32[]{:S(2)}, u32[]{:S(2)}) async-start(bf16[8,256,2,256]{3,1,2,0:T(8,128)(2,1)} %broadcast_select_fusion), calls=%async_computation.1 | async-start | bytes 4194304 | tf_op jit(solution)/shard_map/all_to_all | solution.py:268
  238.8 51.5 %all-to-all-start = ((bf16[8,256,2,256]{3,1,2,0:T(8,128)(2,1)}), bf16[8,256,2,256]{3,1,2,0:T(8,128)(2,1)}, u32[]{:S(2)}, u32[]{:S(2)}) async-start(bf16[8,256,2,256]{3,1,2,0:T(8,128)(2,1)} %broadcast_select_fusion.1), calls=%async_computation | async-start | bytes 4194304 | tf_op jit(solution)/shard_map/all_to_all | solution.py:253
  243.4 4.5 copy-start.18
  247.0 5.8 %copy-start.15 = (f32[128]{0:T(128)S(1)}, f32[128]{0:T(128)}, u32[]{:S(2)}) copy-start(f32[128]{0:T(128)} %param.17) | copy-start | bytes 1540
  335.7 9.1 %copy-start.6 = (f32[2,8,64,64]{2,3,1,0:T(8,128)S(1)}, f32[2,8,64,64]{2,3,1,0:T(8,128)}, u32[]{:S(2)}) copy-start(f32[2,8,64,64]{2,3,1,0:T(8,128)} %get-tuple-element.66) | copy-start | bytes 786436
  335.7 9.2 %copy-start.5 = (bf16[1,4096,1,256]{1,3,2,0:T(8,128)(2,1)S(1)}, bf16[1,4096,1,256]{1,3,2,0:T(8,128)(2,1)}, u32[]{:S(2)}) copy-start(bf16[1,4096,1,256]{1,3,2,0:T(8,128)(2,1)} %copy.65) | copy-start | bytes 6291460
  344.9 7.8 %copy-start.7 = (f32[2,8,64,64]{2,3,1,0:T(8,128)S(1)}, f32[2,8,64,64]{2,3,1,0:T(8,128)}, u32[]{:S(2)}) copy-start(f32[2,8,64,64]{2,3,1,0:T(8,128)} %get-tuple-element.66) | copy-start | bytes 786436
  344.9 8.3 %copy-start.2 = (bf16[2048,640]{1,0:T(8,128)(2,1)S(1)}, bf16[2048,640]{1,0:T(8,128)(2,1)}, u32[]{:S(2)}) copy-start(bf16[2048,640]{1,0:T(8,128)(2,1)} %w_ref.1) | copy-start | bytes 7864324
  344.9 98.1 %copy-start.1 = (bf16[640,2048]{1,0:T(8,128)(2,1)S(1)}, bf16[640,2048]{1,0:T(8,128)(2,1)}, u32[]{:S(2)}) copy-start(bf16[640,2048]{1,0:T(8,128)(2,1)} %param.19) | copy-start | bytes 7864324
Sparse Core Ops, SparseCore 0:
  12.7 70.6 all-gather.4
  85.0 70.1 all-gather.2
